TPU v7x, 256 devices: a whole 4x4x8 slice. The times are simulated.
256 devices in a mesh: own: 8 (over z), col: 8 (over x, core), mlp: 4 (over y).
Axes of the slice: x: 4, y: 4, z: 8, core: 2. Of those that a mesh axis runs over, the one named last changes fastest.
Arguments:
- features: bfloat16 [262144, 512], P(('own', 'col')), may hold values from -6 to 6
- nbr_page: int32 [8192, 32], P(('own', 'col')), may hold values from 0 to 262143, as said below
- nbr_weight: bfloat16 [8192, 32], P(('own', 'col')), may hold values from 0.0049743652 to 0.29882812
- labels: int32 [8192], P(('own', 'col')), may hold values from 0 to 255
- w_one: bfloat16 [512, 2048], P(None, 'mlp'), may hold values from -0.25 to 0.25
- w_two: bfloat16 [2048, 256], P('mlp'), may hold values from -0.125 to 0.125
Outputs:
- grad_one: float32 [512, 2048], P(None, 'mlp')
- grad_two: float32 [2048, 256], P('mlp')
Inputs may be any that keep to these rules, and one draw needn't show every extreme that they name: `nbr_page`: page p is held by owner p // 4096 (owners numbered along own then col) at its row p % 4096. The 32 neighbours of a target are distinct pages listed in non-decreasing order of owner. Of the 4096 neighbour entries of the targets of one index of own and col, at most 128 fall on one owner; one owner receives exactly 128 entries from every index, and some owners receive none from some indices.
All inputs are finite; a program needn't handle non-finite values.
Results may differ from a plain program's by a relative error of at most 0.011.
Values may be sent and summed in bfloat16 or wider, within the bound.
No kernel may reach another device: no remote copies, remote signals or barrier semaphores. Data moves between devices by JAX's collectives and lax.ppermute only.
A program may use at most 128 MiB of HBM per device.

v0:
```python
import jax
import jax.numpy as jnp
from jax import lax
from jax.sharding import PartitionSpec as P


def body(features, nbr_page, nbr_weight, labels, w_one, w_two):
    rows_dev = features.shape[0]
    width_f = features.shape[1]
    targets = nbr_page.shape[0]
    width_k = nbr_page.shape[1]
    owners = lax.axis_size(("own", "col"))
    entries = targets * width_k
    capacity = 2 * entries // owners
    owner_ids = nbr_page // rows_dev
    local_row = nbr_page % rows_dev
    owner_range = jnp.arange(owners, dtype=jnp.int32)
    matches = (owner_ids[:, :, None] == owner_range[None, None, :]).astype(jnp.int32)
    row_count = jnp.sum(matches, axis=1)
    earlier_rows = jnp.cumsum(row_count, axis=0) - row_count
    before_owner = jnp.cumsum(row_count, axis=1) - row_count
    first_slot = earlier_rows - before_owner + owner_range[None, :] * capacity
    slot_ids = (
        jnp.sum(matches * first_slot[:, None, :], axis=2)
        + jnp.arange(width_k, dtype=jnp.int32)[None, :]
    )
    flat_slot = slot_ids.reshape(-1)
    requests = jnp.zeros((owners * capacity,), jnp.int32).at[flat_slot].set(local_row.reshape(-1))
    requests = requests.reshape(owners, capacity)
    asked_rows = lax.all_to_all(requests, ("own", "col"), split_axis=0, concat_axis=0, tiled=True)
    fetched = features[asked_rows]
    returned = lax.all_to_all(fetched, ("own", "col"), split_axis=0, concat_axis=0, tiled=True)
    received = returned.reshape(owners * capacity, width_f)
    contract_first = (((0,), (0,)), ((), ()))
    target_ids = jnp.broadcast_to(
        jnp.arange(targets, dtype=jnp.int32)[:, None], (targets, width_k)
    ).reshape(-1)
    spread = (
        jnp.zeros((targets, owners * capacity), jnp.bfloat16)
        .at[target_ids, flat_slot]
        .set(nbr_weight.reshape(-1))
    )
    pre_act = jnp.dot(received, w_one, preferred_element_type=jnp.float32)
    active = jnp.maximum(pre_act, 0.0).astype(jnp.bfloat16)
    hidden = jnp.dot(spread, active, preferred_element_type=jnp.float32).astype(jnp.bfloat16)
    partial_logits = jnp.dot(hidden, w_two, preferred_element_type=jnp.float32)
    logits = lax.psum(partial_logits, "mlp")
    exponent = jnp.exp(logits)
    probability = exponent / jnp.sum(exponent, axis=1, keepdims=True)
    classes = w_two.shape[1]
    onehot_label = (labels[:, None] == jnp.arange(classes, dtype=jnp.int32)[None, :]).astype(
        jnp.float32
    )
    d_logits = (probability - onehot_label).astype(jnp.bfloat16)
    grad_two = lax.dot_general(hidden, d_logits, contract_first, preferred_element_type=jnp.float32)
    d_hidden = lax.dot_general(
        d_logits, w_two, (((1,), (1,)), ((), ())), preferred_element_type=jnp.float32
    ).astype(jnp.bfloat16)
    positive = (pre_act > 0).astype(jnp.float32)
    scattered = lax.dot_general(
        spread, d_hidden, contract_first, preferred_element_type=jnp.float32
    )
    d_pre = (scattered * positive).astype(jnp.bfloat16)
    grad_one = lax.dot_general(received, d_pre, contract_first, preferred_element_type=jnp.float32)
    grad_one, grad_two = lax.psum((grad_one, grad_two), ("own", "col"))
    return (grad_one, grad_two)


def solution(mesh):
    placed = (
        P(("own", "col"), None),
        P(("own", "col"), None),
        P(("own", "col"), None),
        P(("own", "col")),
        P(None, "mlp"),
        P("mlp", None),
    )
    return jax.shard_map(
        body,
        mesh=mesh,
        in_specs=placed,
        out_specs=(P(None, "mlp"), P("mlp", None)),
        check_vma=False,
    )
```

profile of v0, /device:TPU:8, one launch (start us, length us, event | category | flops | bytes accessed | tf_op | source)
XLA Modules:
  0.0 551.1 jit_solution(711926448814235918)
XLA Ops:
  7.2 0.8 add_select_fusion
  8.0 0.1 convert_reduce_fusion
  8.2 0.1 reduce_window_sum.23
  8.3 0.1 copy.18
  8.4 0.1 copy.22
  8.6 0.2 reduce_window_sum.22
  8.8 0.2 select_reduce_fusion
  9.1 0.1 copy.21
  9.2 0.1 add.85
  9.4 15.5 %scatter_custom_fusion = s32[8192]{0:T(1024)S(1)} fusion(s32[4096]{0:T(1024)S(1)} %bitcast.22, s32[4096]{0:T(1024)S(1)} %reshape.163, s32[]{:T(128)} %constant.41.clone.1), kind=kCustom, calls=%fused_computation.34 | custom fusion | bytes 32772 | tf_op jit(solution)/shard_map/scatter | solution.py:28
  25.0 21.3 %all_to_all.17 = s32[64,1,128]{2,1,0:T(1,128)S(1)} all-to-all(s32[64,1,128]{2,1,0:T(1,128)S(1)} %bitcast.23), channel_id=1, replica_groups=mesh['own'=8,'col'=8,'mlp'=4] {'own','col'}, dimensions={0} | all-to-all | bytes 65536 | tf_op jit(solution)/shard_map/all_to_all | solution.py:30
  46.3 36.5 %gather_fusion = bf16[8192,512]{1,0:T(8,128)(2,1)} fusion(bf16[4096,512]{1,0:T(8,128)(2,1)} %param.6, s32[8192]{0:T(1024)S(1)} %fusion.7), kind=kCustom, calls=%fused_computation | custom fusion | bytes 16809984 | tf_op jit(solution)/shard_map/gather | solution.py:31
  82.8 5.9 %all-to-all-start.1 = ((bf16[64,128,512]{2,1,0:T(8,128)(2,1)}), bf16[64,128,512]{2,1,0:T(8,128)(2,1)}, u32[]{:S(2)}, u32[]{:S(2)}) async-start(bf16[64,128,512]{2,1,0:T(8,128)(2,1)} %bitcast.21), calls=%async_computation.1 | async-start | bytes 16777216 | tf_op jit(solution)/shard_map/all_to_all | solution.py:32
  88.8 0.1 copy.23
  88.9 0.1 reshape.169
  89.0 0.1 multiply_reduce_fusion
  89.1 0.1 and_reduce_fusion
  89.3 30.4 %scatter_custom_fusion.1 = bf16[1048576]{0:T(1024)(128)(2,1)} fusion(s32[4096]{0:T(1024)S(1)} %broadcast_select_fusion, bf16[4096]{0:T(1024)(128)(2,1)S(1)} %reshape.169, bf16[]{:T(256)} %constant.50.clone.1), kind=kCustom, calls=%fused_computation.10 | custom fusion | bytes 2097154
  119.7 2.8 reshape.150
  122.5 152.3 %all-to-all-done.1 = bf16[64,128,512]{2,1,0:T(8,128)(2,1)} async-done(((bf16[64,128,512]{2,1,0:T(8,128)(2,1)}), bf16[64,128,512]{2,1,0:T(8,128)(2,1)}, u32[]{:S(2)}, u32[]{:S(2)}) %all-to-all-start.1) | async-done | bytes 8388640 | tf_op jit(solution)/shard_map/all_to_all | solution.py:32
  274.8 7.1 %fusion.15 = f32[8192,512]{1,0:T(8,128)S(1)} fusion(bf16[8192,512]{1,0:T(8,128)(2,1)} %bitcast.5, bf16[512,512]{1,0:T(8,128)(2,1)S(1)} %copy-done), kind=kOutput, calls=%fused_computation.43 | convolution fusion | flops 4294967296 | bytes 25690112 | tf_op jit(solution)/shard_map/dot_general | solution.py:43
  281.9 1.6 fusion.3
  283.5 4.1 copy-done.1
  287.6 0.8 fusion.16
  288.5 42.6 %all-reduce.4.cloned.1.call-done = f32[128,256]{1,0:T(8,128)} async-done(((f32[128,256]{1,0:T(8,128)}), f32[128,256]{1,0:T(8,128)}) %all-reduce.4.cloned.1.call-update) | async-done | bytes 131088 | tf_op jit(solution)/shard_map/psum | solution.py:47
  331.1 1.0 exponential_reduce_fusion
  332.1 1.1 convolution_convert_fusion
  333.2 16.1 %fusion.2 = f32[512,512]{1,0:T(8,128)} fusion(bf16[8192,512]{1,0:T(8,128)(2,1)} %bitcast.5, f32[8192,512]{1,0:T(8,128)} %copy-done.1, bf16[128,8192]{1,0:T(8,128)(2,1)S(1)} %reshape.150, bf16[128,512]{1,0:T(8,128)(2,1)S(1)} %convolution_convert_fusion), kind=kOutput, calls=%fused_computation.7 | convolution fusion | flops 5381292032 | bytes 28442624 | tf_op jit(solution)/shard_map/dot_general | solution.py:64
  349.3 1.1 fusion.14
  350.5 189.7 %all-reduce.6.cloned.1.call-done = (f32[512,512]{1,0:T(8,128)}, f32[512,256]{1,0:T(8,128)}) async-done(((f32[512,512]{1,0:T(8,128)}, f32[512,256]{1,0:T(8,128)}), (f32[512,512]{1,0:T(8,128)}, f32[512,256]{1,0:T(8,128)})) %all-reduce.6.cloned.1.call-update) | async-done | bytes 1572880 | tf_op jit(solution)/shard_map/psum | solution.py:65
  540.2 2.3 copy.27
  542.4 1.9 copy.28
  (30 shorter events, 0.6 us)
Async XLA Ops:
  7.2 267.6 %copy-start = (bf16[512,512]{1,0:T(8,128)(2,1)S(1)}, bf16[512,512]{1,0:T(8,128)(2,1)}, u32[]{:S(2)}) copy-start(bf16[512,512]{1,0:T(8,128)(2,1)} %param.10) | copy-start | bytes 1572868
  82.8 6.0 %copy-start.4 = (bf16[128,32]{0,1:T(8,128)(2,1)S(1)}, bf16[128,32]{0,1:T(8,128)(2,1)}, u32[]{:S(2)}) copy-start(bf16[128,32]{0,1:T(8,128)(2,1)} %param.8) | copy-start | bytes 24580
  82.8 6.2 %copy-start.7 = (s32[2]{0:T(128)S(1)}, s32[2]{0:T(128)}, u32[]{:S(2)}) copy-start(s32[2]{0:T(128)} %constant.51) | copy-start | bytes 28
  82.8 6.3 %copy-start.6 = (s32[2]{0:T(128)S(1)}, s32[2]{0:T(128)}, u32[]{:S(2)}) copy-start(s32[2]{0:T(128)} %constant.54) | copy-start | bytes 28
  82.8 191.9 %all-to-all-start.1 = ((bf16[64,128,512]{2,1,0:T(8,128)(2,1)}), bf16[64,128,512]{2,1,0:T(8,128)(2,1)}, u32[]{:S(2)}, u32[]{:S(2)}) async-start(bf16[64,128,512]{2,1,0:T(8,128)(2,1)} %bitcast.21), calls=%async_computation.1 | async-start | bytes 16777216 | tf_op jit(solution)/shard_map/all_to_all | solution.py:32
  88.7 242.3 %all-reduce.4.cloned.1.call-start = ((), (), s32[]{:S(2)}) async-start(), calls=%async_computation.2 | async-start | bytes 262144 | tf_op jit(solution)/shard_map/psum | solution.py:47
  281.9 5.7 %copy-start.1 = (f32[8192,512]{1,0:T(8,128)}, f32[8192,512]{1,0:T(8,128)S(1)}, u32[]{:S(2)}) copy-start(f32[8192,512]{1,0:T(8,128)S(1)} %fusion.15) | copy-start | bytes 50331652
  281.9 5.7 %copy-start.3 = (bf16[512,256]{1,0:T(8,128)(2,1)S(1)}, bf16[512,256]{1,0:T(8,128)(2,1)}, u32[]{:S(2)}) copy-start(bf16[512,256]{1,0:T(8,128)(2,1)} %param.11) | copy-start | bytes 786436
  281.9 50.2 %copy-start.5 = (s32[128]{0:T(128)S(1)}, s32[128]{0:T(128)}, u32[]{:S(2)}) copy-start(s32[128]{0:T(128)} %param.9) | copy-start | bytes 1540
  288.5 251.7 %all-reduce.6.cloned.1.call-start = ((), (), s32[]{:S(2)}) async-start(), calls=%async_computation.3 | async-start | bytes 3145728 | tf_op jit(solution)/shard_map/psum | solution.py:65
  333.2 16.1 %copy-start.2 = (f32[128,256]{1,0:T(8,128)S(1)}, f32[128,256]{1,0:T(8,128)}, u32[]{:S(2)}) copy-start(f32[128,256]{1,0:T(8,128)} %all-reduce.4.cloned.1.call-done) | copy-start | bytes 393220
Sparse Core Ops, SparseCore 0:
  288.6 42.4 all-reduce.3
  350.6 189.5 all-reduce.5
where the time goes:
time: 552 us; the launch traced here: 551 us
  waiting for transfers between devices  385 us (70%)
  local copies, waits for them, and re-layouts  94.5 us (17%)
  matrix products  27.8 us (5%)
  blocking collectives  21.3 us (4%)
  between operations  14.3 us (3%)
  starting transfers between devices  5.97 us (1%)
    psum x1, waiting for transfers between devices, body(): grad_one, grad_two = lax.psum((grad_one, grad_two), ('own', 'col'))  190 us
    all_to_all x1, waiting for transfers between devices, body(): lax.all_to_all(fetched, ('own', 'col'), split_axis=0, concat_axis=0, tile...  152 us
    psum x1, waiting for transfers between devices, body(): logits = lax.psum(partial_logits, 'mlp')  42.6 us
    unnamed x20, local copies, waits for them, and re-layouts  38.8 us
    gather x1, local copies, waits for them, and re-layouts, body(): fetched = features[asked_rows]  36.5 us
    all_to_all x1, blocking collectives, body(): lax.all_to_all(requests, ('own', 'col'), split_axis=0, concat_axis=0, til...  21.3 us
    dot_general x1, matrix products, body(): lax.dot_general(received, d_pre, contract_first, preferred_element_type=j...  16.1 us
    scatter x1, local copies, waits for them, and re-layouts, body(): jnp.zeros((owners * capacity,), jnp.int32).at[flat_slot]  15.5 us
  transfers between devices with their start and end apart: 3, of which 3 were waited for; matrix products, arithmetic and copies ran while one was open for 6% of the time, Pallas kernels for 0%

commit v1 on v0

--- a/solution.py
+++ b/solution.py
@@ -62,7 +62,7 @@
     )
     d_pre = (scattered * positive).astype(jnp.bfloat16)
     grad_one = lax.dot_general(received, d_pre, contract_first, preferred_element_type=jnp.float32)
-    grad_one, grad_two = lax.psum((grad_one, grad_two), ("own", "col"))
+    grad_one, grad_two = lax.psum(lax.psum((grad_one, grad_two), "col"), "own")
     return (grad_one, grad_two)
 
 

time: 552 us -> 513 us (0.929)
  waiting for transfers between devices: 385 us -> 347 us
    psum x1 -> x2, waiting for transfers between devices: 190 us -> 152 us  [body(): grad_one, grad_two = lax.psum(lax.psum((grad_one, grad_two), 'col'), 'own')]
  transfers between devices with their start and end apart: 3 -> 4, of which waited for: 3 -> 4; matrix products, arithmetic and copies ran while one was open for 6% -> 7% of each run, Pallas kernels for 0% -> 0%
where the time goes in v1:
time: 513 us
  waiting for transfers between devices  347 us (68%)
  local copies, waits for them, and re-layouts  94.5 us (18%)
  matrix products  27.8 us (5%)
  blocking collectives  21.3 us (4%)
  between operations  14 us (3%)
  starting transfers between devices  6.01 us (1%)
    all_to_all x1, waiting for transfers between devices, body(): lax.all_to_all(fetched, ('own', 'col'), split_axis=0, concat_axis=0, tile...  152 us
    psum x2, waiting for transfers between devices, body(): grad_one, grad_two = lax.psum(lax.psum((grad_one, grad_two), 'col'), 'own')  152 us
    psum x1, waiting for transfers between devices, body(): logits = lax.psum(partial_logits, 'mlp')  42.6 us
    unnamed x20, local copies, waits for them, and re-layouts  38.8 us
    gather x1, local copies, waits for them, and re-layouts, body(): fetched = features[asked_rows]  36.5 us
    all_to_all x1, blocking collectives, body(): lax.all_to_all(requests, ('own', 'col'), split_axis=0, concat_axis=0, til...  21.3 us
    dot_general x1, matrix products, body(): lax.dot_general(received, d_pre, contract_first, preferred_element_type=j...  16.1 us
    scatter x1, local copies, waits for them, and re-layouts, body(): jnp.zeros((owners * capacity,), jnp.int32).at[flat_slot]  15.5 us
  transfers between devices with their start and end apart: 4, of which 4 were waited for; matrix products, arithmetic and copies ran while one was open for 7% of the time, Pallas kernels for 0%

profile of v1, /device:TPU:8, one launch (start us, length us, event | category | flops | bytes accessed | tf_op | source)
XLA Modules:
  0.0 512.9 jit_solution(6544283634433122361)
XLA Ops:
  7.2 0.8 add_select_fusion
  8.0 0.1 convert_reduce_fusion
  8.2 0.1 reduce_window_sum.23
  8.4 0.1 copy.22
  8.6 0.2 reduce_window_sum.22
  8.8 0.2 select_reduce_fusion
  9.1 0.1 copy.21
  9.2 0.1 add.89
  9.4 15.5 %scatter_custom_fusion = s32[8192]{0:T(1024)S(1)} fusion(s32[4096]{0:T(1024)S(1)} %bitcast.22, s32[4096]{0:T(1024)S(1)} %reshape.163, s32[]{:T(128)} %constant.41.clone.1), kind=kCustom, calls=%fused_computation.34 | custom fusion | bytes 32772 | tf_op jit(solution)/shard_map/scatter | solution.py:28
  25.0 21.3 %all_to_all.17 = s32[64,1,128]{2,1,0:T(1,128)S(1)} all-to-all(s32[64,1,128]{2,1,0:T(1,128)S(1)} %bitcast.23), channel_id=1, replica_groups=mesh['own'=8,'col'=8,'mlp'=4] {'own','col'}, dimensions={0} | all-to-all | bytes 65536 | tf_op jit(solution)/shard_map/all_to_all | solution.py:30
  46.3 36.5 %gather_fusion = bf16[8192,512]{1,0:T(8,128)(2,1)} fusion(bf16[4096,512]{1,0:T(8,128)(2,1)} %param.6, s32[8192]{0:T(1024)S(1)} %fusion.7), kind=kCustom, calls=%fused_computation | custom fusion | bytes 16809984 | tf_op jit(solution)/shard_map/gather | solution.py:31
  82.8 5.9 %all-to-all-start.1 = ((bf16[64,128,512]{2,1,0:T(8,128)(2,1)}), bf16[64,128,512]{2,1,0:T(8,128)(2,1)}, u32[]{:S(2)}, u32[]{:S(2)}) async-start(bf16[64,128,512]{2,1,0:T(8,128)(2,1)} %bitcast.21), calls=%async_computation.1 | async-start | bytes 16777216 | tf_op jit(solution)/shard_map/all_to_all | solution.py:32
  88.8 0.1 copy.23
  88.9 0.1 reshape.169
  89.0 0.1 multiply_reduce_fusion
  89.1 0.1 and_reduce_fusion
  89.3 30.4 %scatter_custom_fusion.1 = bf16[1048576]{0:T(1024)(128)(2,1)} fusion(s32[4096]{0:T(1024)S(1)} %broadcast_select_fusion, bf16[4096]{0:T(1024)(128)(2,1)S(1)} %reshape.169, bf16[]{:T(256)} %constant.50.clone.1), kind=kCustom, calls=%fused_computation.10 | custom fusion | bytes 2097154
  119.7 2.8 reshape.150
  122.5 152.3 %all-to-all-done.1 = bf16[64,128,512]{2,1,0:T(8,128)(2,1)} async-done(((bf16[64,128,512]{2,1,0:T(8,128)(2,1)}), bf16[64,128,512]{2,1,0:T(8,128)(2,1)}, u32[]{:S(2)}, u32[]{:S(2)}) %all-to-all-start.1) | async-done | bytes 8388640 | tf_op jit(solution)/shard_map/all_to_all | solution.py:32
  274.8 7.1 %fusion.15 = f32[8192,512]{1,0:T(8,128)S(1)} fusion(bf16[8192,512]{1,0:T(8,128)(2,1)} %bitcast.5, bf16[512,512]{1,0:T(8,128)(2,1)S(1)} %copy-done), kind=kOutput, calls=%fused_computation.43 | convolution fusion | flops 4294967296 | bytes 25690112 | tf_op jit(solution)/shard_map/dot_general | solution.py:43
  281.9 1.6 fusion.3
  283.5 4.1 copy-done.1
  287.6 0.8 fusion.16
  288.5 42.6 %all-reduce.6.cloned.1.call-done = f32[128,256]{1,0:T(8,128)} async-done(((f32[128,256]{1,0:T(8,128)}), f32[128,256]{1,0:T(8,128)}) %all-reduce.6.cloned.1.call-update) | async-done | bytes 131088 | tf_op jit(solution)/shard_map/psum | solution.py:47
  331.1 1.0 exponential_reduce_fusion
  332.1 1.1 convolution_convert_fusion
  333.2 16.1 %fusion.2 = f32[512,512]{1,0:T(8,128)} fusion(bf16[8192,512]{1,0:T(8,128)(2,1)} %bitcast.5, f32[8192,512]{1,0:T(8,128)} %copy-done.1, bf16[128,8192]{1,0:T(8,128)(2,1)S(1)} %reshape.150, bf16[128,512]{1,0:T(8,128)(2,1)S(1)} %convolution_convert_fusion), kind=kOutput, calls=%fused_computation.7 | convolution fusion | flops 5381292032 | bytes 28442624 | tf_op jit(solution)/shard_map/dot_general | solution.py:64
  349.3 1.1 fusion.14
  350.5 70.9 %all-reduce.8.cloned.1.call-done = (f32[512,512]{1,0:T(8,128)}, f32[512,256]{1,0:T(8,128)}) async-done(((f32[512,512]{1,0:T(8,128)}, f32[512,256]{1,0:T(8,128)}), (f32[512,512]{1,0:T(8,128)}, f32[512,256]{1,0:T(8,128)})) %all-reduce.8.cloned.1.call-update) | async-done | bytes 1572880 | tf_op jit(solution)/shard_map/psum | solution.py:65
  421.4 80.8 %all-reduce.10.cloned.1.call-done = (f32[512,512]{1,0:T(8,128)}, f32[512,256]{1,0:T(8,128)}) async-done(((f32[512,512]{1,0:T(8,128)}, f32[512,256]{1,0:T(8,128)}), (f32[512,512]{1,0:T(8,128)}, f32[512,256]{1,0:T(8,128)})) %all-reduce.10.cloned.1.call-update) | async-done | bytes 1572880 | tf_op jit(solution)/shard_map/psum | solution.py:65
  502.2 2.3 copy.29
  504.5 1.9 copy.30
  (33 shorter events, 0.7 us)
Async XLA Ops:
  7.2 267.6 %copy-start = (bf16[512,512]{1,0:T(8,128)(2,1)S(1)}, bf16[512,512]{1,0:T(8,128)(2,1)}, u32[]{:S(2)}) copy-start(bf16[512,512]{1,0:T(8,128)(2,1)} %param.10) | copy-start | bytes 1572868
  82.8 6.0 %copy-start.4 = (bf16[128,32]{0,1:T(8,128)(2,1)S(1)}, bf16[128,32]{0,1:T(8,128)(2,1)}, u32[]{:S(2)}) copy-start(bf16[128,32]{0,1:T(8,128)(2,1)} %param.8) | copy-start | bytes 24580
  82.8 6.2 %copy-start.7 = (s32[2]{0:T(128)S(1)}, s32[2]{0:T(128)}, u32[]{:S(2)}) copy-start(s32[2]{0:T(128)} %constant.51) | copy-start | bytes 28
  82.8 6.3 %copy-start.6 = (s32[2]{0:T(128)S(1)}, s32[2]{0:T(128)}, u32[]{:S(2)}) copy-start(s32[2]{0:T(128)} %constant.54) | copy-start | bytes 28
  82.8 191.9 %all-to-all-start.1 = ((bf16[64,128,512]{2,1,0:T(8,128)(2,1)}), bf16[64,128,512]{2,1,0:T(8,128)(2,1)}, u32[]{:S(2)}, u32[]{:S(2)}) async-start(bf16[64,128,512]{2,1,0:T(8,128)(2,1)} %bitcast.21), calls=%async_computation.1 | async-start | bytes 16777216 | tf_op jit(solution)/shard_map/all_to_all | solution.py:32
  88.7 242.3 %all-reduce.6.cloned.1.call-start = ((), (), s32[]{:S(2)}) async-start(), calls=%async_computation.2 | async-start | bytes 262144 | tf_op jit(solution)/shard_map/psum | solution.py:47
  281.9 5.7 %copy-start.1 = (f32[8192,512]{1,0:T(8,128)}, f32[8192,512]{1,0:T(8,128)S(1)}, u32[]{:S(2)}) copy-start(f32[8192,512]{1,0:T(8,128)S(1)} %fusion.15) | copy-start | bytes 50331652
  281.9 5.7 %copy-start.3 = (bf16[512,256]{1,0:T(8,128)(2,1)S(1)}, bf16[512,256]{1,0:T(8,128)(2,1)}, u32[]{:S(2)}) copy-start(bf16[512,256]{1,0:T(8,128)(2,1)} %param.11) | copy-start | bytes 786436
  281.9 50.2 %copy-start.5 = (s32[128]{0:T(128)S(1)}, s32[128]{0:T(128)}, u32[]{:S(2)}) copy-start(s32[128]{0:T(128)} %param.9) | copy-start | bytes 1540
  288.5 132.9 %all-reduce.8.cloned.1.call-start = ((), (), s32[]{:S(2)}) async-start(), calls=%async_computation.3 | async-start | bytes 3145728 | tf_op jit(solution)/shard_map/psum | solution.py:65
  333.2 16.1 %copy-start.2 = (f32[128,256]{1,0:T(8,128)S(1)}, f32[128,256]{1,0:T(8,128)}, u32[]{:S(2)}) copy-start(f32[128,256]{1,0:T(8,128)} %all-reduce.6.cloned.1.call-done) | copy-start | bytes 393220
  350.5 151.8 %all-reduce.10.cloned.1.call-start = ((), (), s32[]{:S(2)}) async-start(), calls=%async_computation.4 | async-start | bytes 3145728 | tf_op jit(solution)/shard_map/psum | solution.py:65
Sparse Core Ops, SparseCore 0:
  288.6 42.4 all-reduce.5
  350.6 70.7 all-reduce.7
  424.0 78.2 all-reduce.9
